TPU v7x, 512 devices: a whole 4x8x8 slice. The times are simulated.
512 devices in a mesh: rep: 8 (over z_hi, core), row: 8 (over z_lo, x), col: 8 (over y).
Axes of the slice: x: 4, y: 8, z: 8 (z_hi: 4, z_lo: 2; z = z_hi * 2 + z_lo), core: 2. Of those that a mesh axis runs over, the one named last changes fastest.
Arguments:
- inputs: bfloat16 [8, 128, 6144], P('rep', 'col', 'row'), may hold values from -6 to 6
- w_in: bfloat16 [6144, 24576], P('row', ('rep', 'col')), may hold values from -0.078125 to 0.078125
- w_out: bfloat16 [24576, 6144], P(('rep', 'col'), 'row'), may hold values from -0.0390625 to 0.0390625
- cotangent: bfloat16 [8, 128, 6144], P('rep', 'col', 'row'), may hold values from -3072 to 3072
- counts: int32 [8], replicated, may hold values from 0 to 4, as said below
Outputs:
- block_output: bfloat16 [8, 128, 6144], P('rep', 'col', 'row')
- input_grad: bfloat16 [8, 128, 6144], P('rep', 'col', 'row')
- w_in_grad: float32 [6144, 24576], P('row', ('rep', 'col'))
- w_out_grad: float32 [24576, 6144], P(('rep', 'col'), 'row')
Inputs may be any that keep to these rules, and one draw needn't show every extreme that they name: Replica r completed its first counts[r] micro-batches; at least one replica completed all 4.
All inputs are finite; a program needn't handle non-finite values.
Results may differ from a plain program's by a relative error of at most 0.015.
Values may be sent and summed in bfloat16 or wider, within the bound.
No kernel may reach another device: no remote copies, remote signals or barrier semaphores. Data moves between devices by JAX's collectives and lax.ppermute only.
A program may use at most 64 MiB of HBM per device.

v0:
```python
import jax
import jax.numpy as jnp
from jax import lax
from jax.sharding import PartitionSpec as P

MBT = 32
root_coef = 0.7978845608028654
cubic_coef = 0.044715


def in_one_piece(arrays, axis, dim, along):
    both = jnp.concatenate(arrays, axis=along)
    result, at, finished = (lax.all_gather(both, axis, axis=dim, tiled=True), 0, [])
    for a in arrays:
        finished.append(lax.slice_in_dim(result, at, at + a.shape[along], axis=along))
        at += a.shape[along]
    return tuple(finished)


def split_up(value, dim, size):
    dims = value.shape
    pieces = value.reshape(*dims[:dim], size, dims[dim] // size, *dims[dim + 1 :])
    return jnp.moveaxis(pieces, dim, 0)


def summed_on_arrival(value, axis, dim):
    size = lax.axis_size(axis)
    pieces = lax.all_to_all(split_up(value, dim, size), axis, 0, 0, tiled=True)
    return jnp.sum(pieces.astype(jnp.float32), axis=0)


def sent_to_all(value, axis):
    size = lax.axis_size(axis)
    return lax.all_to_all(
        jnp.broadcast_to(value[None], (size, *value.shape)), axis, 0, 0, tiled=True
    )


def joined_along(pieces, dim):
    pieces = jnp.moveaxis(pieces, 0, dim)
    dims = pieces.shape
    return pieces.reshape(*dims[:dim], dims[dim] * dims[dim + 1], *dims[dim + 2 :])


def gathered_copies(value, axis, dim):
    pieces = sent_to_all(value, axis)
    return joined_along(pieces, dim)


def gelu_tanh(values):
    inner = root_coef * (values + cubic_coef * values * values * values)
    return 0.5 * values * (1.0 + jnp.tanh(inner))


def gelu_slope(values):
    inner = root_coef * (values + cubic_coef * values * values * values)
    tangent = jnp.tanh(inner)
    return 0.5 * (1.0 + tangent) + 0.5 * values * (1.0 - tangent * tangent) * root_coef * (
        1.0 + 3.0 * cubic_coef * values * values
    )


def right_product(left, right):
    return lax.dot_general(
        left, right, (((1,), (1,)), ((), ())), preferred_element_type=jnp.float32
    )


def first_product(left, right):
    return lax.dot_general(
        left, right, (((0,), (0,)), ((), ())), preferred_element_type=jnp.float32
    )


def body(inputs, w_in, w_out, cotangent, counts):
    rows_local = inputs.shape[1]
    width_local = inputs.shape[2]
    tokens_local = inputs.reshape(rows_local, width_local)
    replicas = lax.axis_size("rep")
    replica_index = lax.axis_index("rep")
    column_index = lax.axis_index("col")
    own_count = jnp.sum(jnp.where(jnp.arange(replicas) == replica_index, counts, 0))
    token_total = (MBT * jnp.sum(counts)).astype(jnp.float32)
    positions = column_index * rows_local + jnp.arange(rows_local, dtype=jnp.int32)
    kept_mask = (positions // MBT < own_count).astype(jnp.float32)
    scaled = (
        cotangent.reshape(rows_local, width_local).astype(jnp.float32)
        * kept_mask[:, None]
        / token_total
    ).astype(jnp.bfloat16)
    tokens_all, scaled_all = in_one_piece((tokens_local, scaled), "col", 0, 1)
    inner_cols = lax.all_gather(w_in, "rep", axis=1, tiled=True)
    outer_rows = lax.all_gather(w_out, "rep", axis=0, tiled=True)
    partial_hidden = jnp.dot(tokens_all, inner_cols, preferred_element_type=jnp.float32)
    hidden = summed_on_arrival(partial_hidden.astype(jnp.bfloat16), "row", 0)
    active_share = gelu_tanh(hidden).astype(jnp.bfloat16)
    activated = gathered_copies(active_share, "row", 0)
    output_terms = jnp.dot(activated, outer_rows, preferred_element_type=jnp.float32)
    output_local = summed_on_arrival(output_terms.astype(jnp.bfloat16), "col", 0)
    block_output = (tokens_local.astype(jnp.float32) + output_local).astype(jnp.bfloat16)
    slope_terms = right_product(scaled_all, outer_rows)
    slope_sum = summed_on_arrival(slope_terms.astype(jnp.bfloat16), "row", 0)
    grad_share = (slope_sum * gelu_slope(hidden)).astype(jnp.bfloat16)
    hidden_grad = gathered_copies(grad_share, "row", 0)
    back_terms = right_product(hidden_grad, inner_cols)
    back_local = summed_on_arrival(back_terms.astype(jnp.bfloat16), "col", 0)
    input_grad = (scaled.astype(jnp.float32) + back_local).astype(jnp.bfloat16)
    token_reps, scaled_reps = in_one_piece((tokens_all, scaled_all), "rep", 0, 1)
    hidden_reps, active_reps = (
        lax.all_to_all(hidden_grad, "rep", split_axis=1, concat_axis=0, tiled=True),
        lax.all_to_all(activated, "rep", split_axis=1, concat_axis=0, tiled=True),
    )
    w_in_grad = first_product(token_reps, hidden_reps)
    w_out_grad = first_product(active_reps, scaled_reps)
    return (
        block_output.reshape(1, rows_local, width_local),
        input_grad.reshape(1, rows_local, width_local),
        w_in_grad,
        w_out_grad,
    )


def solution(mesh):
    placed = (
        P("rep", "col", "row"),
        P("row", ("rep", "col")),
        P(("rep", "col"), "row"),
        P("rep", "col", "row"),
        P(),
    )
    return jax.shard_map(
        body,
        mesh=mesh,
        in_specs=placed,
        out_specs=(
            P("rep", "col", "row"),
            P("rep", "col", "row"),
            P("row", ("rep", "col")),
            P(("rep", "col"), "row"),
        ),
        check_vma=False,
    )
```

profile of v0, /device:TPU:2, one launch (start us, length us, event | category | flops | bytes accessed | tf_op | source)
XLA Modules:
  0.0 305.8 jit_solution(1008410382800476033)
XLA Ops:
  7.2 0.0 all-gather.6.cloned.1.call-start
  7.2 0.7 all-gather.6.cloned.1.call-update
  7.9 0.0 all-gather.4.cloned.1.call-start
  7.9 0.7 all-gather.4.cloned.1.call-update
  8.7 1.3 fusion.20
  10.6 0.7 compare_convert_fusion
  11.3 0.8 fusion.15
  12.1 0.7 pad_maximum_fusion
  12.8 26.6 %all_gather.12 = bf16[128,1536]{1,0:T(8,128)(2,1)S(1)} all-gather(bf16[16,1536]{1,0:T(8,128)(2,1)S(1)} %pad_maximum_fusion), channel_id=1, replica_groups=mesh['rep'=8,'row'=8,'col'=8] {'col'}, dimensions={0}, use_global_device_ids=true | all-gather | bytes 442368 | tf_op jit(solution)/shard_map/all_gather | solution.py:13
  39.4 35.9 %all-gather.6.cloned.1.call-done = bf16[3072,768]{1,0:T(8,128)(2,1)} async-done(((bf16[384,768]{1,0:T(8,128)(2,1)}), bf16[3072,768]{1,0:T(8,128)(2,1)}) %all-gather.6.cloned.1.call-update) | async-done | bytes 4718608 | tf_op jit(solution)/shard_map/all_gather | solution.py:93
  75.3 4.9 %convolution_convert_fusion = bf16[128,3072]{1,0:T(8,128)(2,1)} fusion(bf16[3072,768]{1,0:T(8,128)(2,1)} %all-gather.6.cloned.1.call-done, bf16[128,1536]{1,0:T(8,128)(2,1)S(1)} %all_gather.12), kind=kOutput, calls=%fused_computation | convolution fusion | flops 604372992 | bytes 5701632 | tf_op jit(solution)/shard_map/dot_general | solution.py:64
  80.2 4.8 %all-to-all-start.3 = ((bf16[8,16,3072]{2,1,0:T(8,128)(2,1)}), bf16[8,16,3072]{2,1,0:T(8,128)(2,1)S(1)}, u32[]{:S(2)}, u32[]{:S(2)}) async-start(bf16[8,16,3072]{2,1,0:T(8,128)(2,1)} %bitcast.6), calls=%async_computation.3 | async-start | bytes 1572864 | tf_op jit(solution)/shard_map/all_to_all | solution.py:28
  85.0 53.2 %all-gather.4.cloned.1.call-done = bf16[768,3072]{1,0:T(8,128)(2,1)} async-done(((bf16[768,384]{1,0:T(8,128)(2,1)}), bf16[768,3072]{1,0:T(8,128)(2,1)}) %all-gather.4.cloned.1.call-update) | async-done | bytes 4718608 | tf_op jit(solution)/shard_map/all_gather | solution.py:92
  138.2 0.0 copy-done
  138.2 4.1 %convolution_convert_fusion.1 = bf16[128,3072]{1,0:T(8,128)(2,1)} fusion(bf16[768,3072]{1,0:T(8,128)(2,1)} %all-gather.4.cloned.1.call-done, bf16[128,1536]{1,0:T(8,128)(2,1)S(1)} %all_gather.12), kind=kOutput, calls=%fused_computation.1 | convolution fusion | flops 604372992 | bytes 5701632 | tf_op jit(solution)/shard_map/dot_general | solution.py:94
  142.3 0.0 all-to-all-done.3
  142.3 4.8 %all-to-all-start = ((bf16[8,16,3072]{2,1,0:T(8,128)(2,1)}), bf16[8,16,3072]{2,1,0:T(8,128)(2,1)S(1)}, u32[]{:S(2)}, u32[]{:S(2)}) async-start(bf16[8,16,3072]{2,1,0:T(8,128)(2,1)} %bitcast.2), calls=%async_computation | async-start | bytes 1572864 | tf_op jit(solution)/shard_map/all_to_all | solution.py:28
  147.1 0.1 convert_reduce_fusion
  147.2 11.1 %all-to-all-done = bf16[8,16,3072]{2,1,0:T(8,128)(2,1)S(1)} async-done(((bf16[8,16,3072]{2,1,0:T(8,128)(2,1)}), bf16[8,16,3072]{2,1,0:T(8,128)(2,1)S(1)}, u32[]{:S(2)}, u32[]{:S(2)}) %all-to-all-start) | async-done | bytes 786464 | tf_op jit(solution)/shard_map/all_to_all | solution.py:28
  158.4 0.1 convert_reduce_fusion.1
  158.5 0.1 fusion.10
  158.6 1.0 broadcast_in_dim.9
  159.6 4.8 %all-to-all-start.1 = ((bf16[8,16,3072]{2,1,0:T(8,128)(2,1)}), bf16[8,16,3072]{2,1,0:T(8,128)(2,1)S(1)}, u32[]{:S(2)}, u32[]{:S(2)}) async-start(bf16[8,16,3072]{2,1,0:T(8,128)(2,1)} %broadcast_in_dim.9), calls=%async_computation.1 | async-start | bytes 1572864 | tf_op jit(solution)/shard_map/all_to_all | solution.py:34
  164.4 0.0 all-gather.8.cloned.1.call-start
  164.4 0.7 all-gather.8.cloned.1.call-update
  165.1 10.3 %all-to-all-done.1 = bf16[8,16,3072]{2,1,0:T(8,128)(2,1)S(1)} async-done(((bf16[8,16,3072]{2,1,0:T(8,128)(2,1)}), bf16[8,16,3072]{2,1,0:T(8,128)(2,1)S(1)}, u32[]{:S(2)}, u32[]{:S(2)}) %all-to-all-start.1) | async-done | bytes 786464 | tf_op jit(solution)/shard_map/all_to_all | solution.py:34
  175.4 1.0 broadcast_in_dim.10
  176.3 4.8 %all-to-all-start.4 = ((bf16[8,16,3072]{2,1,0:T(8,128)(2,1)}), bf16[8,16,3072]{2,1,0:T(8,128)(2,1)S(1)}, u32[]{:S(2)}, u32[]{:S(2)}) async-start(bf16[8,16,3072]{2,1,0:T(8,128)(2,1)} %broadcast_in_dim.10), calls=%async_computation.4 | async-start | bytes 1572864 | tf_op jit(solution)/shard_map/all_to_all | solution.py:34
  181.2 3.8 %convolution_convert_fusion.3 = bf16[128,768]{1,0:T(8,128)(2,1)} fusion(bf16[128,3072]{1,0:T(8,128)(2,1)S(1)} %bitcast.43, bf16[3072,768]{1,0:T(8,128)(2,1)} %all-gather.6.cloned.1.call-done), kind=kOutput, calls=%fused_computation.9 | convolution fusion | flops 604078080 | bytes 5701632 | tf_op jit(solution)/shard_map/dot_general | solution.py:98
  185.0 26.9 %all-to-all-done.4 = bf16[8,16,3072]{2,1,0:T(8,128)(2,1)S(1)} async-done(((bf16[8,16,3072]{2,1,0:T(8,128)(2,1)}), bf16[8,16,3072]{2,1,0:T(8,128)(2,1)S(1)}, u32[]{:S(2)}, u32[]{:S(2)}) %all-to-all-start.4) | async-done | bytes 786464 | tf_op jit(solution)/shard_map/all_to_all | solution.py:34
  211.9 6.9 %all-to-all-start.2 = ((bf16[8,16,768]{2,1,0:T(8,128)(2,1)}), bf16[8,16,768]{2,1,0:T(8,128)(2,1)S(1)}, u32[]{:S(2)}, u32[]{:S(2)}) async-start(bf16[8,16,768]{2,1,0:T(8,128)(2,1)} %bitcast.4), calls=%async_computation.2 | async-start | bytes 393216 | tf_op jit(solution)/shard_map/all_to_all | solution.py:28
  218.8 4.7 %convolution_convert_fusion.2 = bf16[128,768]{1,0:T(8,128)(2,1)} fusion(bf16[128,3072]{1,0:T(8,128)(2,1)S(1)} %bitcast.45, bf16[768,3072]{1,0:T(8,128)(2,1)} %all-gather.4.cloned.1.call-done), kind=kOutput, calls=%fused_computation.8 | convolution fusion | flops 604078080 | bytes 5701632 | tf_op jit(solution)/shard_map/dot_general | solution.py:64
  223.5 5.3 %all-to-all-done.2 = bf16[8,16,768]{2,1,0:T(8,128)(2,1)S(1)} async-done(((bf16[8,16,768]{2,1,0:T(8,128)(2,1)}), bf16[8,16,768]{2,1,0:T(8,128)(2,1)S(1)}, u32[]{:S(2)}, u32[]{:S(2)}) %all-to-all-start.2) | async-done | bytes 196640 | tf_op jit(solution)/shard_map/all_to_all | solution.py:28
  228.7 3.4 %all-to-all-start.5 = ((bf16[8,16,768]{2,1,0:T(8,128)(2,1)}), bf16[8,16,768]{2,1,0:T(8,128)(2,1)S(1)}, u32[]{:S(2)}, u32[]{:S(2)}) async-start(bf16[8,16,768]{2,1,0:T(8,128)(2,1)} %bitcast.8), calls=%async_computation.5 | async-start | bytes 393216 | tf_op jit(solution)/shard_map/all_to_all | solution.py:28
  232.1 0.1 copy.13
  232.3 1.0 copy.11
  233.3 8.6 %all-to-all-done.5 = bf16[8,16,768]{2,1,0:T(8,128)(2,1)S(1)} async-done(((bf16[8,16,768]{2,1,0:T(8,128)(2,1)}), bf16[8,16,768]{2,1,0:T(8,128)(2,1)S(1)}, u32[]{:S(2)}, u32[]{:S(2)}) %all-to-all-start.5) | async-done | bytes 196640 | tf_op jit(solution)/shard_map/all_to_all | solution.py:28
  241.8 3.5 %all-to-all-start.6 = ((bf16[128,8,384]{2,0,1:T(8,128)(2,1)}), bf16[128,8,384]{2,0,1:T(8,128)(2,1)S(1)}, u32[]{:S(2)}, u32[]{:S(2)}) async-start(bf16[128,8,384]{2,0,1:T(8,128)(2,1)} %copy.11), calls=%async_computation.6 | async-start | bytes 1572864 | tf_op jit(solution)/shard_map/all_to_all | solution.py:110
  245.4 0.1 copy.14
  245.5 1.0 copy.12
  246.5 22.3 %all-to-all-done.6 = bf16[128,8,384]{2,0,1:T(8,128)(2,1)S(1)} async-done(((bf16[128,8,384]{2,0,1:T(8,128)(2,1)}), bf16[128,8,384]{2,0,1:T(8,128)(2,1)S(1)}, u32[]{:S(2)}, u32[]{:S(2)}) %all-to-all-start.6) | async-done | bytes 786464 | tf_op jit(solution)/shard_map/all_to_all | solution.py:110
  268.8 3.5 %all-to-all-start.7 = ((bf16[128,8,384]{2,0,1:T(8,128)(2,1)}), bf16[128,8,384]{2,0,1:T(8,128)(2,1)S(1)}, u32[]{:S(2)}, u32[]{:S(2)}) async-start(bf16[128,8,384]{2,0,1:T(8,128)(2,1)} %copy.12), calls=%async_computation.7 | async-start | bytes 1572864 | tf_op jit(solution)/shard_map/all_to_all | solution.py:111
  272.4 0.0 copy-done.2
  272.5 0.6 fusion.19
  273.1 0.7 fusion.18
  273.8 3.4 %fusion.2 = f32[768,384]{1,0:T(8,128)} fusion(bf16[1024,384]{1,0:T(8,128)(2,1)S(1)} %bitcast.49, bf16[1024,1536]{1,0:T(8,128)(2,1)} %all-gather.8.cloned.1.call-done), kind=kOutput, calls=%fused_computation.4 | convolution fusion | flops 603979776 | bytes 3538944 | tf_op jit(solution)/shard_map/dot_general | solution.py:70
  277.2 18.9 %all-to-all-done.7 = bf16[128,8,384]{2,0,1:T(8,128)(2,1)S(1)} async-done(((bf16[128,8,384]{2,0,1:T(8,128)(2,1)}), bf16[128,8,384]{2,0,1:T(8,128)(2,1)S(1)}, u32[]{:S(2)}, u32[]{:S(2)}) %all-to-all-start.7) | async-done | bytes 786464 | tf_op jit(solution)/shard_map/all_to_all | solution.py:111
  296.1 3.2 %fusion = f32[384,768]{1,0:T(8,128)} fusion(bf16[1024,384]{1,0:T(8,128)(2,1)S(1)} %bitcast.50, bf16[1024,1536]{1,0:T(8,128)(2,1)} %all-gather.8.cloned.1.call-done), kind=kOutput, calls=%fused_computation.2 | convolution fusion | flops 603979776 | bytes 3538944 | tf_op jit(solution)/shard_map/dot_general | solution.py:70
  (7 shorter events, 0.1 us)
Async XLA Ops:
  7.2 68.2 %all-gather.6.cloned.1.call-start = ((), (), s32[]{:S(2)}) async-start(), calls=%async_computation.9 | async-start | bytes 5308416 | tf_op jit(solution)/shard_map/all_gather | solution.py:93
  7.9 130.3 %all-gather.4.cloned.1.call-start = ((), (), s32[]{:S(2)}) async-start(), calls=%async_computation.8 | async-start | bytes 5308416 | tf_op jit(solution)/shard_map/all_gather | solution.py:92
  39.4 98.8 %copy-start = (bf16[128,1536]{1,0:T(8,128)(2,1)}, bf16[128,1536]{1,0:T(8,128)(2,1)S(1)}, u32[]{:S(2)}) copy-start(bf16[128,1536]{1,0:T(8,128)(2,1)S(1)} %all_gather.12) | copy-start | bytes 1179652
  80.2 62.1 %all-to-all-start.3 = ((bf16[8,16,3072]{2,1,0:T(8,128)(2,1)}), bf16[8,16,3072]{2,1,0:T(8,128)(2,1)S(1)}, u32[]{:S(2)}, u32[]{:S(2)}) async-start(bf16[8,16,3072]{2,1,0:T(8,128)(2,1)} %bitcast.6), calls=%async_computation.3 | async-start | bytes 1572864 | tf_op jit(solution)/shard_map/all_to_all | solution.py:28
  142.3 16.1 %all-to-all-start = ((bf16[8,16,3072]{2,1,0:T(8,128)(2,1)}), bf16[8,16,3072]{2,1,0:T(8,128)(2,1)S(1)}, u32[]{:S(2)}, u32[]{:S(2)}) async-start(bf16[8,16,3072]{2,1,0:T(8,128)(2,1)} %bitcast.2), calls=%async_computation | async-start | bytes 1572864 | tf_op jit(solution)/shard_map/all_to_all | solution.py:28
  159.6 15.8 %all-to-all-start.1 = ((bf16[8,16,3072]{2,1,0:T(8,128)(2,1)}), bf16[8,16,3072]{2,1,0:T(8,128)(2,1)S(1)}, u32[]{:S(2)}, u32[]{:S(2)}) async-start(bf16[8,16,3072]{2,1,0:T(8,128)(2,1)} %broadcast_in_dim.9), calls=%async_computation.1 | async-start | bytes 1572864 | tf_op jit(solution)/shard_map/all_to_all | solution.py:34
  164.4 109.4 %all-gather.8.cloned.1.call-start = ((), (), s32[]{:S(2)}) async-start(), calls=%async_computation.10 | async-start | bytes 3538944 | tf_op jit(solution)/shard_map/all_gather | solution.py:13
  176.3 35.5 %all-to-all-start.4 = ((bf16[8,16,3072]{2,1,0:T(8,128)(2,1)}), bf16[8,16,3072]{2,1,0:T(8,128)(2,1)S(1)}, u32[]{:S(2)}, u32[]{:S(2)}) async-start(bf16[8,16,3072]{2,1,0:T(8,128)(2,1)} %broadcast_in_dim.10), calls=%async_computation.4 | async-start | bytes 1572864 | tf_op jit(solution)/shard_map/all_to_all | solution.py:34
  211.9 16.9 %all-to-all-start.2 = ((bf16[8,16,768]{2,1,0:T(8,128)(2,1)}), bf16[8,16,768]{2,1,0:T(8,128)(2,1)S(1)}, u32[]{:S(2)}, u32[]{:S(2)}) async-start(bf16[8,16,768]{2,1,0:T(8,128)(2,1)} %bitcast.4), calls=%async_computation.2 | async-start | bytes 393216 | tf_op jit(solution)/shard_map/all_to_all | solution.py:28
  228.7 13.1 %all-to-all-start.5 = ((bf16[8,16,768]{2,1,0:T(8,128)(2,1)}), bf16[8,16,768]{2,1,0:T(8,128)(2,1)S(1)}, u32[]{:S(2)}, u32[]{:S(2)}) async-start(bf16[8,16,768]{2,1,0:T(8,128)(2,1)} %bitcast.8), calls=%async_computation.5 | async-start | bytes 393216 | tf_op jit(solution)/shard_map/all_to_all | solution.py:28
  233.3 39.2 %copy-start.2 = (bf16[1,16,768]{2,1,0:T(8,128)(2,1)S(1)}, bf16[1,16,768]{2,1,0:T(8,128)(2,1)}, u32[]{:S(2)}) copy-start(bf16[1,16,768]{2,1,0:T(8,128)(2,1)} %param.5) | copy-start | bytes 73732
  233.3 39.8 %copy-start.1 = (bf16[1,16,768]{2,1,0:T(8,128)(2,1)S(1)}, bf16[1,16,768]{2,1,0:T(8,128)(2,1)}, u32[]{:S(2)}) copy-start(bf16[1,16,768]{2,1,0:T(8,128)(2,1)} %param.8) | copy-start | bytes 73732
  241.8 27.0 %all-to-all-start.6 = ((bf16[128,8,384]{2,0,1:T(8,128)(2,1)}), bf16[128,8,384]{2,0,1:T(8,128)(2,1)S(1)}, u32[]{:S(2)}, u32[]{:S(2)}) async-start(bf16[128,8,384]{2,0,1:T(8,128)(2,1)} %copy.11), calls=%async_computation.6 | async-start | bytes 1572864 | tf_op jit(solution)/shard_map/all_to_all | solution.py:110
  268.8 27.3 %all-to-all-start.7 = ((bf16[128,8,384]{2,0,1:T(8,128)(2,1)}), bf16[128,8,384]{2,0,1:T(8,128)(2,1)S(1)}, u32[]{:S(2)}, u32[]{:S(2)}) async-start(bf16[128,8,384]{2,0,1:T(8,128)(2,1)} %copy.12), calls=%async_computation.7 | async-start | bytes 1572864 | tf_op jit(solution)/shard_map/all_to_all | solution.py:111
Sparse Core Ops, SparseCore 0:
  10.1 65.1 all-gather.5
  77.5 60.7 all-gather.3
  167.3 52.0 all-gather.7
where the time goes:
time: 307 us; the launch traced here: 306 us
  waiting for transfers between devices  195 us (64%)
  starting transfers between devices  36.7 us (12%)
  blocking collectives  26.6 us (9%)
  matrix products  24.1 us (8%)
  between operations  14.5 us (5%)
  other arithmetic  5.26 us (2%)
  local copies, waits for them, and re-layouts  4.15 us (1%)
    all_gather x1, waiting for transfers between devices, body(): inner_cols = lax.all_gather(w_in, 'rep', axis=1, tiled=True)  53.2 us
    all_to_all x2, waiting for transfers between devices, sent_to_all(): lax.all_to_all(jnp.broadcast_to(value[None], (size, *value.shape)), axis,...  37.2 us
    all_gather x1, waiting for transfers between devices, body(): outer_rows = lax.all_gather(w_out, 'rep', axis=0, tiled=True)  35.9 us
    all_gather x1, blocking collectives, in_one_piece(): lax.all_gather(both, axis, axis=dim, tiled=True)  26.6 us
    all_to_all x4, waiting for transfers between devices, summed_on_arrival(): pieces = lax.all_to_all(split_up(value, dim, size), axis, 0, 0, tiled=True)  25 us
    all_to_all x1, waiting for transfers between devices, body(): lax.all_to_all(hidden_grad, 'rep', split_axis=1, concat_axis=0, tiled=True)  22.3 us
    all_to_all x4, starting transfers between devices, summed_on_arrival(): pieces = lax.all_to_all(split_up(value, dim, size), axis, 0, 0, tiled=True)  19.9 us
    all_to_all x1, waiting for transfers between devices, body(): lax.all_to_all(activated, 'rep', split_axis=1, concat_axis=0, tiled=True)  18.9 us
  transfers between devices with their start and end apart: 11, of which 9 were waited for; matrix products, arithmetic and copies ran while one was open for 10% of the time, Pallas kernels for 0%

commit v1 on v0

--- a/solution.py
+++ b/solution.py
@@ -107,7 +107,12 @@
     input_grad = (scaled.astype(jnp.float32) + back_local).astype(jnp.bfloat16)
     token_reps, scaled_reps = in_one_piece((tokens_all, scaled_all), "rep", 0, 1)
     hidden_reps, active_reps = (
-        lax.all_to_all(hidden_grad, "rep", split_axis=1, concat_axis=0, tiled=True),
+        jnp.concatenate(
+            lax.all_to_all(
+                jnp.stack(jnp.split(hidden_grad, lax.axis_size("rep"), axis=1)), "rep", 0, 0
+            ),
+            axis=0,
+        ),
         lax.all_to_all(activated, "rep", split_axis=1, concat_axis=0, tiled=True),
     )
     w_in_grad = first_product(token_reps, hidden_reps)

time: 307 us -> 288 us (0.938)
  the two profiles are of different devices: /device:TPU:2 before, /device:TPU:8 now
where the time goes in v1:
time: 288 us; the launch traced here: 287 us
  waiting for transfers between devices  158 us (55%)
  blocking collectives  44.3 us (15%)
  starting transfers between devices  34 us (12%)
  matrix products  24.1 us (8%)
  between operations  14.5 us (5%)
  local copies, waits for them, and re-layouts  7.34 us (3%)
  other arithmetic  5.26 us (2%)
    all_gather x1, waiting for transfers between devices, body(): inner_cols = lax.all_gather(w_in, 'rep', axis=1, tiled=True)  53.8 us
    all_gather x1, waiting for transfers between devices, body(): outer_rows = lax.all_gather(w_out, 'rep', axis=0, tiled=True)  34.7 us
    all_gather x1, blocking collectives, in_one_piece(): lax.all_gather(both, axis, axis=dim, tiled=True)  27.8 us
    all_to_all x4, starting transfers between devices, summed_on_arrival(): pieces = lax.all_to_all(split_up(value, dim, size), axis, 0, 0, tiled=True)  23 us
    all_to_all x1, waiting for transfers between devices, body(): lax.all_to_all(jnp.stack(jnp.split(hidden_grad, lax.axis_size('rep'), axi...  22.6 us
    all_to_all x4, waiting for transfers between devices, summed_on_arrival(): pieces = lax.all_to_all(split_up(value, dim, size), axis, 0, 0, tiled=True)  19.3 us
    all_to_all x1, waiting for transfers between devices, body(): lax.all_to_all(activated, 'rep', split_axis=1, concat_axis=0, tiled=True)  18.8 us
    all_to_all x1, blocking collectives, sent_to_all(): lax.all_to_all(jnp.broadcast_to(value[None], (size, *value.shape)), axis,...  16.5 us
  transfers between devices with their start and end apart: 10, of which 7 were waited for; matrix products, arithmetic and copies ran while one was open for 11% of the time, Pallas kernels for 0%

profile of v1, /device:TPU:8, one launch (start us, length us, event | category | flops | bytes accessed | tf_op | source)
XLA Modules:
  0.0 287.0 jit_solution(9471991098341842959)
XLA Ops:
  7.2 0.7 all-gather.6.cloned.1.call-update
  7.9 0.0 all-gather.4.cloned.1.call-start
  7.9 0.7 all-gather.4.cloned.1.call-update
  8.7 1.3 fusion.28
  10.6 0.7 compare_convert_fusion
  11.3 0.8 fusion.23
  12.1 0.7 pad_maximum_fusion
  12.8 27.8 %all_gather.12 = bf16[128,1536]{1,0:T(8,128)(2,1)S(1)} all-gather(bf16[16,1536]{1,0:T(8,128)(2,1)S(1)} %pad_maximum_fusion), channel_id=1, replica_groups=mesh['rep'=8,'row'=8,'col'=8] {'col'}, dimensions={0}, use_global_device_ids=true | all-gather | bytes 442368 | tf_op jit(solution)/shard_map/all_gather | solution.py:13
  40.6 34.7 %all-gather.6.cloned.1.call-done = bf16[3072,768]{1,0:T(8,128)(2,1)} async-done(((bf16[384,768]{1,0:T(8,128)(2,1)}), bf16[3072,768]{1,0:T(8,128)(2,1)}) %all-gather.6.cloned.1.call-update) | async-done | bytes 4718608 | tf_op jit(solution)/shard_map/all_gather | solution.py:93
  75.3 4.9 %convolution_convert_fusion = bf16[128,3072]{1,0:T(8,128)(2,1)} fusion(bf16[3072,768]{1,0:T(8,128)(2,1)} %all-gather.6.cloned.1.call-done, bf16[128,1536]{1,0:T(8,128)(2,1)S(1)} %all_gather.12), kind=kOutput, calls=%fused_computation | convolution fusion | flops 604372992 | bytes 5701632 | tf_op jit(solution)/shard_map/dot_general | solution.py:64
  80.2 4.3 %all-to-all-start.3 = ((bf16[8,16,3072]{2,1,0:T(8,128)(2,1)}), bf16[8,16,3072]{2,1,0:T(8,128)(2,1)S(1)}, u32[]{:S(2)}, u32[]{:S(2)}) async-start(bf16[8,16,3072]{2,1,0:T(8,128)(2,1)} %bitcast.6), calls=%async_computation.3 | async-start | bytes 1572864 | tf_op jit(solution)/shard_map/all_to_all | solution.py:28
  84.4 53.8 %all-gather.4.cloned.1.call-done = bf16[768,3072]{1,0:T(8,128)(2,1)} async-done(((bf16[768,384]{1,0:T(8,128)(2,1)}), bf16[768,3072]{1,0:T(8,128)(2,1)}) %all-gather.4.cloned.1.call-update) | async-done | bytes 4718608 | tf_op jit(solution)/shard_map/all_gather | solution.py:92
  138.2 4.1 %convolution_convert_fusion.1 = bf16[128,3072]{1,0:T(8,128)(2,1)} fusion(bf16[768,3072]{1,0:T(8,128)(2,1)} %all-gather.4.cloned.1.call-done, bf16[128,1536]{1,0:T(8,128)(2,1)S(1)} %all_gather.12), kind=kOutput, calls=%fused_computation.1 | convolution fusion | flops 604372992 | bytes 5701632 | tf_op jit(solution)/shard_map/dot_general | solution.py:94
  142.3 4.2 %all-to-all-start = ((bf16[8,16,3072]{2,1,0:T(8,128)(2,1)}), bf16[8,16,3072]{2,1,0:T(8,128)(2,1)S(1)}, u32[]{:S(2)}, u32[]{:S(2)}) async-start(bf16[8,16,3072]{2,1,0:T(8,128)(2,1)} %bitcast.2), calls=%async_computation | async-start | bytes 1572864 | tf_op jit(solution)/shard_map/all_to_all | solution.py:28
  146.5 0.1 convert_reduce_fusion
  146.6 12.3 %all-to-all-done = bf16[8,16,3072]{2,1,0:T(8,128)(2,1)S(1)} async-done(((bf16[8,16,3072]{2,1,0:T(8,128)(2,1)}), bf16[8,16,3072]{2,1,0:T(8,128)(2,1)S(1)}, u32[]{:S(2)}, u32[]{:S(2)}) %all-to-all-start) | async-done | bytes 786464 | tf_op jit(solution)/shard_map/all_to_all | solution.py:28
  158.9 0.1 convert_reduce_fusion.1
  159.0 0.1 fusion.10
  159.2 0.1 broadcast_in_dim.9
  159.3 16.5 %all_to_all.54 = bf16[8,16,3072]{2,1,0:T(8,128)(2,1)S(1)} all-to-all(bf16[8,16,3072]{2,1,0:T(8,128)(2,1)S(1)} %broadcast_in_dim.9), channel_id=1, replica_groups=mesh['rep'=8,'row'=8,'col'=8] {'row'}, dimensions={0} | all-to-all | bytes 1572864 | tf_op jit(solution)/shard_map/all_to_all | solution.py:34
  175.8 1.0 broadcast_in_dim.10
  176.7 3.5 %all-to-all-start.4 = ((bf16[8,16,3072]{2,1,0:T(8,128)(2,1)}), bf16[8,16,3072]{2,1,0:T(8,128)(2,1)S(1)}, u32[]{:S(2)}, u32[]{:S(2)}) async-start(bf16[8,16,3072]{2,1,0:T(8,128)(2,1)} %broadcast_in_dim.10), calls=%async_computation.4 | async-start | bytes 1572864 | tf_op jit(solution)/shard_map/all_to_all | solution.py:34
  180.3 0.0 all-gather.8.cloned.1.call-start
  180.4 0.7 all-gather.8.cloned.1.call-update
  181.0 3.8 %convolution_convert_fusion.3 = bf16[128,768]{1,0:T(8,128)(2,1)} fusion(bf16[128,3072]{1,0:T(8,128)(2,1)S(1)} %bitcast.70, bf16[3072,768]{1,0:T(8,128)(2,1)} %all-gather.6.cloned.1.call-done), kind=kOutput, calls=%fused_computation.9 | convolution fusion | flops 604078080 | bytes 5701632 | tf_op jit(solution)/shard_map/dot_general | solution.py:98
  184.9 6.3 %all-to-all-done.4 = bf16[8,16,3072]{2,1,0:T(8,128)(2,1)S(1)} async-done(((bf16[8,16,3072]{2,1,0:T(8,128)(2,1)}), bf16[8,16,3072]{2,1,0:T(8,128)(2,1)S(1)}, u32[]{:S(2)}, u32[]{:S(2)}) %all-to-all-start.4) | async-done | bytes 786464 | tf_op jit(solution)/shard_map/all_to_all | solution.py:34
  191.2 7.3 %all-to-all-start.2 = ((bf16[8,16,768]{2,1,0:T(8,128)(2,1)}), bf16[8,16,768]{2,1,0:T(8,128)(2,1)S(1)}, u32[]{:S(2)}, u32[]{:S(2)}) async-start(bf16[8,16,768]{2,1,0:T(8,128)(2,1)} %bitcast.4), calls=%async_computation.2 | async-start | bytes 393216 | tf_op jit(solution)/shard_map/all_to_all | solution.py:28
  198.5 0.6 fusion.20
  199.1 0.6 fusion.19
  199.8 0.6 fusion.18
  200.4 0.6 fusion.17
  201.1 0.6 fusion.16
  201.7 0.6 fusion.15
  202.4 4.7 %convolution_convert_fusion.2 = bf16[128,768]{1,0:T(8,128)(2,1)} fusion(bf16[128,3072]{1,0:T(8,128)(2,1)S(1)} %bitcast.78, bf16[768,3072]{1,0:T(8,128)(2,1)} %all-gather.4.cloned.1.call-done), kind=kOutput, calls=%fused_computation.8 | convolution fusion | flops 604078080 | bytes 5701632 | tf_op jit(solution)/shard_map/dot_general | solution.py:64
  207.1 7.2 %all-to-all-start.5 = ((bf16[8,16,768]{2,1,0:T(8,128)(2,1)}), bf16[8,16,768]{2,1,0:T(8,128)(2,1)S(1)}, u32[]{:S(2)}, u32[]{:S(2)}) async-start(bf16[8,16,768]{2,1,0:T(8,128)(2,1)} %bitcast.8), calls=%async_computation.5 | async-start | bytes 393216 | tf_op jit(solution)/shard_map/all_to_all | solution.py:28
  214.3 0.6 fusion.14
  214.9 0.6 fusion.13
  215.6 7.0 %all-to-all-done.5 = bf16[8,16,768]{2,1,0:T(8,128)(2,1)S(1)} async-done(((bf16[8,16,768]{2,1,0:T(8,128)(2,1)}), bf16[8,16,768]{2,1,0:T(8,128)(2,1)S(1)}, u32[]{:S(2)}, u32[]{:S(2)}) %all-to-all-start.5) | async-done | bytes 196640 | tf_op jit(solution)/shard_map/all_to_all | solution.py:28
  222.6 3.8 %all-to-all-start.6 = ((bf16[8,128,384]{2,1,0:T(8,128)(2,1)}), bf16[8,128,384]{2,1,0:T(8,128)(2,1)S(1)}, u32[]{:S(2)}, u32[]{:S(2)}) async-start(bf16[8,128,384]{2,1,0:T(8,128)(2,1)} %fusion.13), calls=%async_computation.6 | async-start | bytes 1572864 | tf_op jit(solution)/shard_map/all_to_all | solution.py:111
  226.4 0.1 copy.11
  226.6 1.0 copy.10
  227.5 22.6 %all-to-all-done.6 = bf16[8,128,384]{2,1,0:T(8,128)(2,1)S(1)} async-done(((bf16[8,128,384]{2,1,0:T(8,128)(2,1)}), bf16[8,128,384]{2,1,0:T(8,128)(2,1)S(1)}, u32[]{:S(2)}, u32[]{:S(2)}) %all-to-all-start.6) | async-done | bytes 786464 | tf_op jit(solution)/shard_map/all_to_all | solution.py:111
  250.1 3.5 %all-to-all-start.7 = ((bf16[128,8,384]{2,0,1:T(8,128)(2,1)}), bf16[128,8,384]{2,0,1:T(8,128)(2,1)S(1)}, u32[]{:S(2)}, u32[]{:S(2)}) async-start(bf16[128,8,384]{2,0,1:T(8,128)(2,1)} %copy.10), calls=%async_computation.7 | async-start | bytes 1572864 | tf_op jit(solution)/shard_map/all_to_all | solution.py:116
  253.8 0.6 fusion.27
  254.4 0.7 fusion.26
  255.1 3.4 %fusion.2 = f32[768,384]{1,0:T(8,128)} fusion(bf16[1024,384]{1,0:T(8,128)(2,1)S(1)} %bitcast.82, bf16[1024,1536]{1,0:T(8,128)(2,1)} %all-gather.8.cloned.1.call-done), kind=kOutput, calls=%fused_computation.4 | convolution fusion | flops 603979776 | bytes 3538944 | tf_op jit(solution)/shard_map/dot_general | solution.py:70
  258.5 18.8 %all-to-all-done.7 = bf16[128,8,384]{2,0,1:T(8,128)(2,1)S(1)} async-done(((bf16[128,8,384]{2,0,1:T(8,128)(2,1)}), bf16[128,8,384]{2,0,1:T(8,128)(2,1)S(1)}, u32[]{:S(2)}, u32[]{:S(2)}) %all-to-all-start.7) | async-done | bytes 786464 | tf_op jit(solution)/shard_map/all_to_all | solution.py:116
  277.3 3.2 %fusion = f32[384,768]{1,0:T(8,128)} fusion(bf16[1024,384]{1,0:T(8,128)(2,1)S(1)} %bitcast.83, bf16[1024,1536]{1,0:T(8,128)(2,1)} %all-gather.8.cloned.1.call-done), kind=kOutput, calls=%fused_computation.2 | convolution fusion | flops 603979776 | bytes 3538944 | tf_op jit(solution)/shard_map/dot_general | solution.py:70
  (12 shorter events, 0.1 us)
Async XLA Ops:
  7.2 68.1 %all-gather.6.cloned.1.call-start = ((), (), s32[]{:S(2)}) async-start(), calls=%async_computation.9 | async-start | bytes 5308416 | tf_op jit(solution)/shard_map/all_gather | solution.py:93
  7.9 130.3 %all-gather.4.cloned.1.call-start = ((), (), s32[]{:S(2)}) async-start(), calls=%async_computation.8 | async-start | bytes 5308416 | tf_op jit(solution)/shard_map/all_gather | solution.py:92
  40.6 97.6 %copy-start = (bf16[128,1536]{1,0:T(8,128)(2,1)}, bf16[128,1536]{1,0:T(8,128)(2,1)S(1)}, u32[]{:S(2)}) copy-start(bf16[128,1536]{1,0:T(8,128)(2,1)S(1)} %all_gather.12) | copy-start | bytes 1179652
  80.2 62.1 %all-to-all-start.3 = ((bf16[8,16,3072]{2,1,0:T(8,128)(2,1)}), bf16[8,16,3072]{2,1,0:T(8,128)(2,1)S(1)}, u32[]{:S(2)}, u32[]{:S(2)}) async-start(bf16[8,16,3072]{2,1,0:T(8,128)(2,1)} %bitcast.6), calls=%async_computation.3 | async-start | bytes 1572864 | tf_op jit(solution)/shard_map/all_to_all | solution.py:28
  142.3 16.6 %all-to-all-start = ((bf16[8,16,3072]{2,1,0:T(8,128)(2,1)}), bf16[8,16,3072]{2,1,0:T(8,128)(2,1)S(1)}, u32[]{:S(2)}, u32[]{:S(2)}) async-start(bf16[8,16,3072]{2,1,0:T(8,128)(2,1)} %bitcast.2), calls=%async_computation | async-start | bytes 1572864 | tf_op jit(solution)/shard_map/all_to_all | solution.py:28
  176.7 14.4 %all-to-all-start.4 = ((bf16[8,16,3072]{2,1,0:T(8,128)(2,1)}), bf16[8,16,3072]{2,1,0:T(8,128)(2,1)S(1)}, u32[]{:S(2)}, u32[]{:S(2)}) async-start(bf16[8,16,3072]{2,1,0:T(8,128)(2,1)} %broadcast_in_dim.10), calls=%async_computation.4 | async-start | bytes 1572864 | tf_op jit(solution)/shard_map/all_to_all | solution.py:34
  180.3 74.8 %all-gather.8.cloned.1.call-start = ((), (), s32[]{:S(2)}) async-start(), calls=%async_computation.10 | async-start | bytes 3538944 | tf_op jit(solution)/shard_map/all_gather | solution.py:13
  191.2 15.9 %all-to-all-start.2 = ((bf16[8,16,768]{2,1,0:T(8,128)(2,1)}), bf16[8,16,768]{2,1,0:T(8,128)(2,1)S(1)}, u32[]{:S(2)}, u32[]{:S(2)}) async-start(bf16[8,16,768]{2,1,0:T(8,128)(2,1)} %bitcast.4), calls=%async_computation.2 | async-start | bytes 393216 | tf_op jit(solution)/shard_map/all_to_all | solution.py:28
  207.1 15.5 %all-to-all-start.5 = ((bf16[8,16,768]{2,1,0:T(8,128)(2,1)}), bf16[8,16,768]{2,1,0:T(8,128)(2,1)S(1)}, u32[]{:S(2)}, u32[]{:S(2)}) async-start(bf16[8,16,768]{2,1,0:T(8,128)(2,1)} %bitcast.8), calls=%async_computation.5 | async-start | bytes 393216 | tf_op jit(solution)/shard_map/all_to_all | solution.py:28
  215.6 38.2 %copy-start.2 = (bf16[1,16,768]{2,1,0:T(8,128)(2,1)S(1)}, bf16[1,16,768]{2,1,0:T(8,128)(2,1)}, u32[]{:S(2)}) copy-start(bf16[1,16,768]{2,1,0:T(8,128)(2,1)} %param.5) | copy-start | bytes 73732
  215.6 38.8 %copy-start.1 = (bf16[1,16,768]{2,1,0:T(8,128)(2,1)S(1)}, bf16[1,16,768]{2,1,0:T(8,128)(2,1)}, u32[]{:S(2)}) copy-start(bf16[1,16,768]{2,1,0:T(8,128)(2,1)} %param.8) | copy-start | bytes 73732
  222.6 27.5 %all-to-all-start.6 = ((bf16[8,128,384]{2,1,0:T(8,128)(2,1)}), bf16[8,128,384]{2,1,0:T(8,128)(2,1)S(1)}, u32[]{:S(2)}, u32[]{:S(2)}) async-start(bf16[8,128,384]{2,1,0:T(8,128)(2,1)} %fusion.13), calls=%async_computation.6 | async-start | bytes 1572864 | tf_op jit(solution)/shard_map/all_to_all | solution.py:111
  250.1 27.1 %all-to-all-start.7 = ((bf16[128,8,384]{2,0,1:T(8,128)(2,1)}), bf16[128,8,384]{2,0,1:T(8,128)(2,1)S(1)}, u32[]{:S(2)}, u32[]{:S(2)}) async-start(bf16[128,8,384]{2,0,1:T(8,128)(2,1)} %copy.10), calls=%async_computation.7 | async-start | bytes 1572864 | tf_op jit(solution)/shard_map/all_to_all | solution.py:116
Sparse Core Ops, SparseCore 0:
  10.1 65.1 all-gather.5
  77.4 60.7 all-gather.3
  183.3 45.8 all-gather.7
